TPU v7x, 128 devices: a whole 4x4x4 slice. The times are simulated.
128 devices in a mesh: row: 16 (over y_lo, x, core), col: 8 (over y_hi, z).
Axes of the slice: x: 4, y: 4 (y_hi: 2, y_lo: 2; y = y_hi * 2 + y_lo), z: 4, core: 2. Of those that a mesh axis runs over, the one named last changes fastest.
Arguments:
- eigvecs: float32 [8, 256, 131072], P('col', 'row'), may hold values from -6 to 6
- reflectors: float32 [8, 131072, 256], P('col', 'row'), may hold values from -6 to 6
- factors: float32 [8, 256, 256], P('col'), may hold values from -7.6293945e-06 to 3.0517578e-05, as said below
- owner: int32 [8], replicated, may hold values from 0 to 7, each once
Outputs:
- back_vectors: float32 [8, 256, 131072], P('col', None, 'row')
Inputs may be any that keep to these rules, and one draw needn't show every extreme that they name: Each factors[c] is upper triangular with a positive diagonal.
All inputs are finite; a program needn't handle non-finite values.
Results may differ from a plain program's by a relative error of at most 0.0001.
Values sent between devices are 32-bit elements; how exact they have to be, the bound alone decides.
No kernel may reach another device: no remote copies, remote signals or barrier semaphores. Data moves between devices by JAX's collectives and lax.ppermute only.
A program may use at most 192 MiB of HBM per device.

v0:
```python
import jax
import jax.numpy as jnp
from jax import lax
from jax.sharding import PartitionSpec as P


def from_root(value, axis, source):
    kept = jnp.where(lax.axis_index(axis) == source, value, 0).astype(value.dtype)
    return lax.psum(kept, axis)


def times(left, right):
    return lax.dot_general(
        left,
        right,
        (((1,), (0,)), ((), ())),
        precision=lax.Precision.HIGHEST,
        preferred_element_type=jnp.float32,
    )


def times_rows(left, right):
    return lax.dot_general(
        left,
        right,
        (((1,), (1,)), ((), ())),
        precision=lax.Precision.HIGHEST,
        preferred_element_type=jnp.float32,
    )


def shards(eigvecs, reflectors, factors, owner):
    groups = lax.axis_size("row")
    own_count = eigvecs.shape[1]
    rows_here = eigvecs.shape[2] // groups
    split_vecs = eigvecs.reshape(own_count, groups, rows_here)
    local = lax.all_to_all(split_vecs, "row", split_axis=1, concat_axis=0, tiled=True)
    field = local.reshape(own_count * groups, rows_here)
    width = factors.shape[1]
    offset = lax.axis_index("row") * rows_here
    for block in (1, 0):
        vectors = from_root(reflectors, "col", owner[block])
        factor = from_root(factors, "col", owner[block])
        rows = offset + lax.broadcasted_iota(jnp.int32, (rows_here, width), 0)
        cols = lax.broadcasted_iota(jnp.int32, (rows_here, width), 1) + block * width
        masked = jnp.where(rows > cols, vectors[0], jnp.zeros_like(vectors[0]))
        masked = masked + (rows == cols).astype(jnp.float32)
        vectors, factor = (masked, factor[0])
        project = lax.psum(times(field, vectors), "row")
        update = times_rows(project, factor)
        field = field - times_rows(update, vectors)
    return field[None]


def solution(mesh):
    in_specs = (P("col", "row", None), P("col", "row", None), P("col", None, None), P())
    out_specs = P("col", None, "row")
    return jax.shard_map(shards, mesh=mesh, in_specs=in_specs, out_specs=out_specs, check_vma=False)
```

profile of v0, /device:TPU:1, one launch (start us, length us, event | category | flops | bytes accessed | tf_op | source)
XLA Modules:
  0.0 772.6 jit_solution(14178438249363084464)
XLA Ops:
  6.5 0.0 all-reduce.9.cloned.1.call-start
  6.5 1.4 fusion.31
  9.2 0.0 copy-start.3
  9.2 10.2 %select_bitcast_fusion = (f32[8192,256]{1,0:T(8,128)}, f32[1,8192,256]{2,1,0:T(8,128)}) fusion(f32[1,8192,256]{2,1,0:T(8,128)} %param.5, pred[]{:T(512)S(6)} %eq.26, pred[]{:T(512)S(6)} %eq.23), kind=kLoop, calls=%fused_computation.9 | loop fusion | flops 4194304 | bytes 25165826 | tf_op jit(solution)/shard_map/squeeze | solution.py:46
  19.4 0.0 copy-done.3
  19.4 0.8 select_bitcast_fusion.1
  20.3 0.0 all-reduce.9.cloned.1.call-update
  20.3 8.2 %copy.6 = f32[2,8,16,8192]{3,2,1,0:T(8,128)S(1)} copy(f32[2,8,16,8192]{3,1,2,0:T(8,128)} %bitcast.41) | data formatting | bytes 16777216
  28.5 8.3 %copy.5 = f32[16,16,8192]{2,0,1:T(8,128)} copy(f32[16,16,8192]{2,1,0:T(8,128)S(1)} %bitcast.40) | data formatting | bytes 16777216 | tf_op jit(solution)/shard_map/reshape | solution.py:36
  36.8 6.8 all-to-all-start
  43.6 0.2 all-reduce.5.cloned.1.call-start
  43.9 115.5 %all-to-all-done = f32[16,16,8192]{2,0,1:T(8,128)} async-done(((f32[16,16,8192]{2,0,1:T(8,128)}), f32[16,16,8192]{2,0,1:T(8,128)}, u32[]{:S(2)}, u32[]{:S(2)}) %all-to-all-start) | async-done | bytes 8388640 | tf_op jit(solution)/shard_map/all_to_all | solution.py:37
  159.3 309.3 %all-reduce.9.cloned.1.call-done = (f32[1,8192,256]{2,1,0:T(8,128)}, f32[256,256]{1,0:T(8,128)}, f32[8192,256]{1,0:T(8,128)}, f32[256,256]{1,0:T(8,128)}) async-done(((f32[1,8192,256]{2,1,0:T(8,128)}, f32[256,256]{1,0:T(8,128)}, f32[8192,256]{1,0:T(8,128)}, f32[256,256]{1,0:T(8,128)}), (f32[1,8192,256]{2,1,0:T(8,128)}, f32[256,256]{1,0:T(8,128)}, f32[8192,256]{1,0:T(8,128)}, ...) | async-done | bytes 17301520 | tf_op jit(solution)/shard_map/psum | solution.py:9
  468.6 0.0 copy-start.2
  468.6 21.6 %fusion.24 = f32[256,256]{0,1:T(8,128)} fusion(f32[256,8192]{1,0:T(8,128)} %bitcast.2, f32[1,8192,256]{2,1,0:T(8,128)} %get-tuple-element.5, s32[256]{0:T(256)S(1)} %iota_add_fusion.1, s32[8192]{0:T(1024)S(1)} %iota_add_fusion), kind=kOutput, calls=%fused_computation.31 | convolution fusion | flops 6452936704 | bytes 17073152 | tf_op jit(solution)/shard_map/dot_general | solution.py:13
  490.2 0.0 all-reduce.5.cloned.1.call-update
  490.2 0.0 all-reduce.7.cloned.1.call-start
  490.2 113.8 %all-reduce.5.cloned.1.call-done = f32[256,256]{0,1:T(8,128)} async-done(((f32[256,256]{0,1:T(8,128)}), f32[256,256]{0,1:T(8,128)}) %all-reduce.5.cloned.1.call-update) | async-done | bytes 262160 | tf_op jit(solution)/shard_map/psum | solution.py:49
  604.0 0.0 copy-done.2
  604.0 0.0 slice-start
  604.0 1.7 fusion.32
  605.7 0.0 slice-start.1
  605.7 13.7 %convolution_subtract_fusion.1 = f32[256,8192]{1,0:T(8,128)S(1)} fusion(f32[256,8192]{1,0:T(8,128)} %bitcast.2, f32[256,256]{1,0:T(8,128)S(1)} %fusion.32, f32[1,8192,256]{2,1,0:T(8,128)} %get-tuple-element.5, s32[256]{0:T(256)S(1)} %iota_add_fusion.1, s32[8192]{0:T(1024)S(1)} %iota_add_fusion), kind=kOutput, calls=%fused_computation.2 | convolution fusion | flops 6455033856 | bytes 25461760 | tf_op jit(solution)/shard_map/dot_general | solution.py:23
  619.4 0.0 copy-start
  619.4 3.4 copy-done
  622.8 0.0 slice-done
  622.8 0.0 slice-done.1
  622.8 0.0 copy-start.1
  622.8 9.2 %fusion.13 = f32[256,256]{1,0:T(8,128)} fusion(f32[256,8192]{1,0:T(8,128)S(1)} %convolution_subtract_fusion.1, f32[8192,256]{1,0:T(8,128)S(1)} %bitcast.39, s32[8192]{0:T(1024)S(1)} %iota_add_fusion), kind=kOutput, calls=%fused_computation.19 | convolution fusion | flops 6452936704 | bytes 17072128 | tf_op jit(solution)/shard_map/dot_general | solution.py:13
  632.0 0.0 all-reduce.7.cloned.1.call-update
  632.1 117.7 %all-reduce.7.cloned.1.call-done = f32[256,256]{1,0:T(8,128)} async-done(((f32[256,256]{1,0:T(8,128)}), f32[256,256]{1,0:T(8,128)}) %all-reduce.7.cloned.1.call-update) | async-done | bytes 262160 | tf_op jit(solution)/shard_map/psum | solution.py:49
  749.7 0.0 copy-done.1
  749.7 1.4 fusion.33
  751.1 14.4 %fusion = f32[1,256,8192]{2,1,0:T(8,128)} fusion(f32[256,8192]{1,0:T(8,128)} %copy-done, f32[256,256]{1,0:T(8,128)S(1)} %fusion.33, f32[8192,256]{1,0:T(8,128)} %get-tuple-element.7, s32[8192]{0:T(1024)S(1)} %iota_add_fusion), kind=kOutput, calls=%fused_computation.1 | convolution fusion | flops 6455033856 | bytes 25460736 | tf_op jit(solution)/shard_map/dot_general | solution.py:23
  (3 shorter events, 0.0 us)
Async XLA Ops:
  6.5 462.1 %all-reduce.9.cloned.1.call-start = ((), (), s32[]{:S(2)}) async-start(), calls=%async_computation.3 | async-start | bytes 34603008 | tf_op jit(solution)/shard_map/psum | solution.py:9
  9.2 10.2 %copy-start.3 = (f32[1,256,256]{2,1,0:T(8,128)S(1)}, f32[1,256,256]{2,1,0:T(8,128)}, u32[]{:S(2)}) copy-start(f32[1,256,256]{2,1,0:T(8,128)} %param.6) | copy-start | bytes 786436
  36.8 122.5 %all-to-all-start = ((f32[16,16,8192]{2,0,1:T(8,128)}), f32[16,16,8192]{2,0,1:T(8,128)}, u32[]{:S(2)}, u32[]{:S(2)}) async-start(f32[16,16,8192]{2,0,1:T(8,128)} %copy.5), calls=%async_computation | async-start | bytes 16777216 | tf_op jit(solution)/shard_map/all_to_all | solution.py:37
  43.6 560.4 %all-reduce.5.cloned.1.call-start = ((), (), s32[]{:S(2)}) async-start(), calls=%async_computation.1 | async-start | bytes 524288 | tf_op jit(solution)/shard_map/psum | solution.py:49
  468.6 135.4 %copy-start.2 = (f32[256,256]{1,0:T(8,128)S(1)}, f32[256,256]{1,0:T(8,128)}, u32[]{:S(2)}) copy-start(f32[256,256]{1,0:T(8,128)} %get-tuple-element.6) | copy-start | bytes 786436
  490.2 259.5 %all-reduce.7.cloned.1.call-start = ((), (), s32[]{:S(2)}) async-start(), calls=%async_computation.2 | async-start | bytes 524288 | tf_op jit(solution)/shard_map/psum | solution.py:49
  604.0 18.8 %slice-start = ((s8[8388608]{0:T(1024)(128)(4,1)}), s8[4194304]{0:T(1024)(128)(4,1)S(1)}, s32[]{:S(2)}) async-start(s8[8388608]{0:T(1024)(128)(4,1)} %bitcast.38), calls=%async_computation.4 | async-start | bytes 8388608
  605.7 17.1 %slice-start.1 = ((s8[8388608]{0:T(1024)(128)(4,1)}), s8[4194304]{0:T(1024)(128)(4,1)S(1)}, s32[]{:S(2)}) async-start(s8[8388608]{0:T(1024)(128)(4,1)} %bitcast.38), calls=%async_computation.5 | async-start | bytes 8388608
  619.4 3.4 copy-start
  622.8 126.9 %copy-start.1 = (f32[256,256]{1,0:T(8,128)S(1)}, f32[256,256]{1,0:T(8,128)}, u32[]{:S(2)}) copy-start(f32[256,256]{1,0:T(8,128)} %get-tuple-element.8) | copy-start | bytes 786436
Sparse Core Ops, SparseCore 0:
  20.4 448.1 all-reduce.8
  490.3 113.6 all-reduce.4
  632.2 117.5 all-reduce.6
where the time goes:
time: 781 us; the launch traced here: 773 us
  waiting for transfers between devices  656 us (84%)
  matrix products  61.9 us (8%)
  local copies, waits for them, and re-layouts  21.3 us (3%)
  between operations  15 us (2%)
  other arithmetic  11.1 us (1%)
    psum x1, waiting for transfers between devices, from_root(): return lax.psum(kept, axis)  309 us
    psum x2, waiting for transfers between devices, shards(): project = lax.psum(times(field, vectors), 'row')  231 us
    all_to_all x1, waiting for transfers between devices, shards(): lax.all_to_all(split_vecs, 'row', split_axis=1, concat_axis=0, tiled=True)  115 us
    dot_general x4, matrix products, times_rows(): lax.dot_general(left, right, (((1,), (1,)), ((), ())), precision=lax.Prec...  31.2 us
    dot_general x2, matrix products, times(): lax.dot_general(left, right, (((1,), (0,)), ((), ())), precision=lax.Prec...  30.8 us
  transfers between devices with their start and end apart: 4, of which 4 were waited for; matrix products, arithmetic and copies ran while one was open for 2% of the time, Pallas kernels for 0%

commit v1 on v0

--- a/solution.py
+++ b/solution.py
@@ -46,7 +46,7 @@
         masked = jnp.where(rows > cols, vectors[0], jnp.zeros_like(vectors[0]))
         masked = masked + (rows == cols).astype(jnp.float32)
         vectors, factor = (masked, factor[0])
-        project = lax.psum(times(field, vectors), "row")
+        project = jnp.sum(lax.all_gather(times(field, vectors), "row"), axis=0)
         update = times_rows(project, factor)
         field = field - times_rows(update, vectors)
     return field[None]

time: 781 us -> 628 us (0.80)
  waiting for transfers between devices: 656 us -> 497 us
    psum x2 -> x0, waiting for transfers between devices: 231 us -> none  [shards(): project = lax.psum(times(field, vectors), 'row')]
    all_gather x0 -> x2, waiting for transfers between devices: none -> 72.6 us  [shards(): project = jnp.sum(lax.all_gather(times(field, vectors), 'row'), axis=0)]
  transfers between devices with their start and end apart: 4 -> 4, of which waited for: 4 -> 4; matrix products, arithmetic and copies ran while one was open for 2% -> 3% of each run, Pallas kernels for 0% -> 0%
where the time goes in v1:
time: 628 us; the launch traced here: 619 us
  waiting for transfers between devices  497 us (79%)
  matrix products  60 us (10%)
  local copies, waits for them, and re-layouts  25.2 us (4%)
  between operations  15 us (2%)
  other arithmetic  14.6 us (2%)
  starting transfers between devices  7.08 us (1%)
    psum x1, waiting for transfers between devices, from_root(): return lax.psum(kept, axis)  309 us
    all_to_all x1, waiting for transfers between devices, shards(): lax.all_to_all(split_vecs, 'row', split_axis=1, concat_axis=0, tiled=True)  115 us
    all_gather x2, waiting for transfers between devices, shards(): project = jnp.sum(lax.all_gather(times(field, vectors), 'row'), axis=0)  72.6 us
    dot_general x2, matrix products, times(): lax.dot_general(left, right, (((1,), (0,)), ((), ())), precision=lax.Prec...  30.7 us
    dot_general x4, matrix products, times_rows(): lax.dot_general(left, right, (((1,), (1,)), ((), ())), precision=lax.Prec...  29.3 us
    unnamed x14, local copies, waits for them, and re-layouts  15.6 us
  transfers between devices with their start and end apart: 4, of which 4 were waited for; matrix products, arithmetic and copies ran while one was open for 3% of the time, Pallas kernels for 0%

profile of v1, /device:TPU:1, one launch (start us, length us, event | category | flops | bytes accessed | tf_op | source)
XLA Modules:
  0.0 619.3 jit_solution(11267530835272518037)
XLA Ops:
  6.5 0.0 all-reduce.3.cloned.1.call-start
  6.5 1.4 fusion.31
  9.2 0.0 copy-start.3
  9.2 10.2 %select_bitcast_fusion = (f32[8192,256]{1,0:T(8,128)}, f32[1,8192,256]{2,1,0:T(8,128)}) fusion(f32[1,8192,256]{2,1,0:T(8,128)} %param.5, pred[]{:T(512)S(6)} %eq.26, pred[]{:T(512)S(6)} %eq.23), kind=kLoop, calls=%fused_computation.9 | loop fusion | flops 4194304 | bytes 25165826 | tf_op jit(solution)/shard_map/squeeze | solution.py:46
  19.4 0.0 copy-done.3
  19.4 0.8 select_bitcast_fusion.1
  20.3 0.0 all-reduce.3.cloned.1.call-update
  20.3 8.2 %copy.7 = f32[2,8,16,8192]{3,2,1,0:T(8,128)S(1)} copy(f32[2,8,16,8192]{3,1,2,0:T(8,128)} %bitcast.47) | data formatting | bytes 16777216
  28.5 8.3 %copy.6 = f32[16,16,8192]{2,0,1:T(8,128)} copy(f32[16,16,8192]{2,1,0:T(8,128)S(1)} %bitcast.46) | data formatting | bytes 16777216 | tf_op jit(solution)/shard_map/reshape | solution.py:36
  36.8 6.8 %all-to-all-start = ((f32[16,16,8192]{2,0,1:T(8,128)}), f32[16,16,8192]{2,0,1:T(8,128)}, u32[]{:S(2)}, u32[]{:S(2)}) async-start(f32[16,16,8192]{2,0,1:T(8,128)} %copy.6), calls=%async_computation | async-start | bytes 16777216 | tf_op jit(solution)/shard_map/all_to_all | solution.py:37
  43.6 0.2 all-gather.5.cloned.1.call-start
  43.9 115.5 %all-to-all-done = f32[16,16,8192]{2,0,1:T(8,128)} async-done(((f32[16,16,8192]{2,0,1:T(8,128)}), f32[16,16,8192]{2,0,1:T(8,128)}, u32[]{:S(2)}, u32[]{:S(2)}) %all-to-all-start) | async-done | bytes 8388640 | tf_op jit(solution)/shard_map/all_to_all | solution.py:37
  159.3 309.3 %all-reduce.3.cloned.1.call-done = (f32[1,8192,256]{2,1,0:T(8,128)}, f32[256,256]{1,0:T(8,128)}, f32[8192,256]{1,0:T(8,128)}, f32[256,256]{1,0:T(8,128)}) async-done(((f32[1,8192,256]{2,1,0:T(8,128)}, f32[256,256]{1,0:T(8,128)}, f32[8192,256]{1,0:T(8,128)}, f32[256,256]{1,0:T(8,128)}), (f32[1,8192,256]{2,1,0:T(8,128)}, f32[256,256]{1,0:T(8,128)}, f32[8192,256]{1,0:T(8,128)}, ...) | async-done | bytes 17301520 | tf_op jit(solution)/shard_map/psum | solution.py:9
  468.6 21.5 %fusion.24 = f32[256,256]{0,1:T(8,128)} fusion(f32[256,8192]{1,0:T(8,128)} %bitcast.2, f32[1,8192,256]{2,1,0:T(8,128)} %get-tuple-element.5, s32[256]{0:T(256)S(1)} %iota_add_fusion.1, s32[8192]{0:T(1024)S(1)} %iota_add_fusion), kind=kOutput, calls=%fused_computation.32 | convolution fusion | flops 6452936704 | bytes 17073152 | tf_op jit(solution)/shard_map/dot_general | solution.py:13
  490.1 0.0 copy-start.2
  490.1 0.0 all-gather.5.cloned.1.call-update
  490.2 0.0 all-gather.7.cloned.1.call-start
  490.2 35.1 %all-gather.5.cloned.1.call-done = f32[4096,256]{0,1:T(8,128)} async-done(((f32[256,256]{0,1:T(8,128)}), f32[4096,256]{0,1:T(8,128)}) %all-gather.5.cloned.1.call-update) | async-done | bytes 4194320 | tf_op jit(solution)/shard_map/all_gather | solution.py:49
  525.3 3.9 copy.8
  529.2 1.0 bitcast_reduce_fusion
  530.2 0.0 copy-done.2
  530.3 0.0 slice-start
  530.3 0.6 fusion.32
  530.9 0.0 slice-start.1
  530.9 13.9 %convolution_subtract_fusion.1 = f32[256,8192]{1,0:T(8,128)S(1)} fusion(f32[256,8192]{1,0:T(8,128)} %bitcast.2, f32[256,256]{1,0:T(8,128)S(1)} %fusion.32, f32[1,8192,256]{2,1,0:T(8,128)} %get-tuple-element.5, s32[256]{0:T(256)S(1)} %iota_add_fusion.1, s32[8192]{0:T(1024)S(1)} %iota_add_fusion), kind=kOutput, calls=%fused_computation.2 | convolution fusion | flops 6455033856 | bytes 25461760 | tf_op jit(solution)/shard_map/dot_general | solution.py:23
  544.7 0.0 copy-start
  544.8 3.4 copy-done
  548.1 0.0 slice-done
  548.1 0.0 slice-done.1
  548.1 0.0 copy-start.1
  548.2 9.2 %fusion.13 = f32[256,256]{1,0:T(8,128)} fusion(f32[256,8192]{1,0:T(8,128)S(1)} %convolution_subtract_fusion.1, f32[8192,256]{1,0:T(8,128)S(1)} %bitcast.45, s32[8192]{0:T(1024)S(1)} %iota_add_fusion), kind=kOutput, calls=%fused_computation.19 | convolution fusion | flops 6452936704 | bytes 17072128 | tf_op jit(solution)/shard_map/dot_general | solution.py:13
  557.4 0.0 all-gather.7.cloned.1.call-update
  557.4 37.6 %all-gather.7.cloned.1.call-done = f32[4096,256]{1,0:T(8,128)} async-done(((f32[256,256]{1,0:T(8,128)}), f32[4096,256]{1,0:T(8,128)}) %all-gather.7.cloned.1.call-update) | async-done | bytes 4194320 | tf_op jit(solution)/shard_map/all_gather | solution.py:49
  595.0 2.5 reduce_sum.19
  597.4 0.0 copy-done.1
  597.5 0.4 fusion.33
  597.9 14.4 %fusion = f32[1,256,8192]{2,1,0:T(8,128)} fusion(f32[256,8192]{1,0:T(8,128)} %copy-done, f32[256,256]{1,0:T(8,128)S(1)} %fusion.33, f32[8192,256]{1,0:T(8,128)} %get-tuple-element.7, s32[8192]{0:T(1024)S(1)} %iota_add_fusion), kind=kOutput, calls=%fused_computation.1 | convolution fusion | flops 6455033856 | bytes 25460736 | tf_op jit(solution)/shard_map/dot_general | solution.py:23
  (3 shorter events, 0.0 us)
Async XLA Ops:
  6.5 462.1 %all-reduce.3.cloned.1.call-start = ((), (), s32[]{:S(2)}) async-start(), calls=%async_computation.3 | async-start | bytes 34603008 | tf_op jit(solution)/shard_map/psum | solution.py:9
  9.2 10.2 %copy-start.3 = (f32[1,256,256]{2,1,0:T(8,128)S(1)}, f32[1,256,256]{2,1,0:T(8,128)}, u32[]{:S(2)}) copy-start(f32[1,256,256]{2,1,0:T(8,128)} %param.6) | copy-start | bytes 786436
  36.8 122.5 %all-to-all-start = ((f32[16,16,8192]{2,0,1:T(8,128)}), f32[16,16,8192]{2,0,1:T(8,128)}, u32[]{:S(2)}, u32[]{:S(2)}) async-start(f32[16,16,8192]{2,0,1:T(8,128)} %copy.6), calls=%async_computation | async-start | bytes 16777216 | tf_op jit(solution)/shard_map/all_to_all | solution.py:37
  43.6 481.7 %all-gather.5.cloned.1.call-start = ((), (), s32[]{:S(2)}) async-start(), calls=%async_computation.1 | async-start | bytes 4456448 | tf_op jit(solution)/shard_map/all_gather | solution.py:49
  490.1 40.1 %copy-start.2 = (f32[256,256]{1,0:T(8,128)S(1)}, f32[256,256]{1,0:T(8,128)}, u32[]{:S(2)}) copy-start(f32[256,256]{1,0:T(8,128)} %get-tuple-element.6) | copy-start | bytes 786436
  490.2 104.8 %all-gather.7.cloned.1.call-start = ((), (), s32[]{:S(2)}) async-start(), calls=%async_computation.2 | async-start | bytes 4456448 | tf_op jit(solution)/shard_map/all_gather | solution.py:49
  530.3 17.9 %slice-start = ((s8[8388608]{0:T(1024)(128)(4,1)}), s8[4194304]{0:T(1024)(128)(4,1)S(1)}, s32[]{:S(2)}) async-start(s8[8388608]{0:T(1024)(128)(4,1)} %bitcast.44), calls=%async_computation.4 | async-start | bytes 8388608
  530.9 17.3 %slice-start.1 = ((s8[8388608]{0:T(1024)(128)(4,1)}), s8[4194304]{0:T(1024)(128)(4,1)S(1)}, s32[]{:S(2)}) async-start(s8[8388608]{0:T(1024)(128)(4,1)} %bitcast.44), calls=%async_computation.5 | async-start | bytes 8388608
  544.7 3.4 copy-start
  548.1 49.3 %copy-start.1 = (f32[256,256]{1,0:T(8,128)S(1)}, f32[256,256]{1,0:T(8,128)}, u32[]{:S(2)}) copy-start(f32[256,256]{1,0:T(8,128)} %get-tuple-element.8) | copy-start | bytes 786436
Sparse Core Ops, SparseCore 0:
  20.4 448.1 all-reduce.2
  490.3 34.9 all-gather.4
  557.5 37.4 all-gather.6
